TPU v7x, 32 devices: a whole 2x2x4 slice. The times are simulated.
32 devices in a mesh: ctx: 4 (over y, x), wa: 8 (over z, core).
Axes of the slice: x: 2, y: 2, z: 4, core: 2. Of those that a mesh axis runs over, the one named last changes fastest.
Arguments:
- block_input: float32 [8, 512, 2048], P('wa', 'ctx'), may hold values from -6 to 6
- query_weight: bfloat16 [2048, 4096], P('wa'), may hold values from -0.125 to 0.125
- key_projection_matrix: bfloat16 [2048, 512], P('wa'), may hold values from -0.125 to 0.125
- value_projection_matrix: bfloat16 [2048, 512], P('wa'), may hold values from -0.125 to 0.125
- output_weight: bfloat16 [4096, 2048], P('wa'), may hold values from -0.1875 to 0.1875
- attention_gain: bfloat16 [2048], P('wa'), may hold values from 0.5 to 1.5
- feedforward_gain: bfloat16 [2048], P('wa'), may hold values from 0.5 to 1.5
- query_gain: bfloat16 [128], P('wa'), may hold values from 0.796875 to 1.296875
- key_gain: bfloat16 [128], P('wa'), may hold values from 0.796875 to 1.296875
- expert_gate: bfloat16 [32, 2048, 768], P(('ctx', 'wa')), may hold values from -0.125 to 0.125
- expert_up: bfloat16 [32, 2048, 768], P(('ctx', 'wa')), may hold values from -0.125 to 0.125
- expert_down: bfloat16 [32, 768, 2048], P(('ctx', 'wa')), may hold values from -0.3125 to 0.3125
- expert_ids: int32 [8, 512, 8], P('wa', 'ctx'), may hold values from 0 to 31, all different within a row; in each aligned block of 128 rows (0 to 127, 128 to 255, ..., all dimensions but the last counted through in order) at most 64 rows name the same one
- route_gates: bfloat16 [8, 512, 8], P('wa', 'ctx'), may hold values from 0.25 to 1
- cotangent: float32 [8, 512, 2048], P('wa', 'ctx'), may hold values from -6 to 6
Outputs:
- block_output: float32 [8, 512, 2048], P('wa', 'ctx')
- input_grad: float32 [8, 512, 2048], P('wa', 'ctx')
- query_weight_grad: float32 [2048, 4096], P('wa')
- key_weight_grad: float32 [2048, 512], P('wa')
- value_weight_grad: float32 [2048, 512], P('wa')
- output_weight_grad: float32 [4096, 2048], P('wa')
- attention_gain_grad: float32 [2048], P('wa')
- feedforward_gain_grad: float32 [2048], P('wa')
- query_gain_grad: float32 [128], P('wa')
- key_gain_grad: float32 [128], P('wa')
- expert_gate_grad: float32 [32, 2048, 768], P(('ctx', 'wa'))
- expert_up_grad: float32 [32, 2048, 768], P(('ctx', 'wa'))
- expert_down_grad: float32 [32, 768, 2048], P(('ctx', 'wa'))
Inputs may be any that keep to these rules, and one draw needn't show every extreme that they name: `expert_ids`: each row names 8 different experts; the rows of one sequence block (128 rows in sequence order) name any one expert at most 64 times, a bound that some block reaches.
All inputs are finite; a program needn't handle non-finite values.
Results may differ from a plain program's by a relative error of at most 0.033.
Values may be sent and summed in bfloat16 or wider, within the bound.
No kernel may reach another device: no remote copies, remote signals or barrier semaphores. Data moves between devices by JAX's collectives and lax.ppermute only.
A program may use at most 320 MiB of HBM per device.

v0:
```python
import jax
import jax.numpy as jnp
from jax import lax
from jax.sharding import PartitionSpec as P

MODEL_WIDTH = 2048
QUERY_HEADS = 32
KEY_VALUE_HEADS = 4
HEAD_SIZE = 128
TOP = 8
EPSILON = 1e-06
ROPE_BASE = 1000000.0
VERY_NEGATIVE = -1e30
EVERY = ("ctx", "wa")


def inv_root(values):
    return lax.rsqrt(jnp.mean(values * values, axis=-1, keepdims=True) + EPSILON)


def rope_tables(positions):
    half_width = HEAD_SIZE // 2
    frequency = ROPE_BASE ** (-(jnp.arange(half_width).astype(positions.dtype) * 2.0 / HEAD_SIZE))
    angles = positions[:, None] * frequency[None, :]
    cosine, sine = (jnp.cos(angles), jnp.sin(angles))
    return (jnp.concatenate([cosine, cosine], axis=-1), jnp.concatenate([-sine, sine], axis=-1))


def swap_halves(values):
    half_width = values.shape[-1] // 2
    return jnp.concatenate([values[..., half_width:], values[..., :half_width]], axis=-1)


def rotate(values, cosine, sine):
    return values * cosine + swap_halves(values) * sine


def unrotate(values, cosine, sine):
    return values * cosine - swap_halves(values) * sine


def dot(a, b, contract):
    return lax.dot_general(a, b, (contract, ((), ())), preferred_element_type=jnp.float32)


def on_device(
    block_input,
    query_weight,
    key_projection_matrix,
    value_projection_matrix,
    output_weight,
    attention_gain,
    feedforward_gain,
    query_gain,
    key_gain,
    expert_gate,
    expert_up,
    expert_down,
    expert_ids,
    route_gates,
    cotangent,
):
    bf16, f32 = (jnp.bfloat16, jnp.float32)
    n_ctx, n_wa = (lax.axis_size("ctx"), lax.axis_size("wa"))
    my_ctx, my_wa = (lax.axis_index("ctx"), lax.axis_index("wa"))
    experts = n_ctx * n_wa
    block_rows = block_input[0]
    rows = block_rows.shape[0]
    length = rows * n_ctx
    capacity = 2 * rows * TOP // experts
    heads = QUERY_HEADS // n_ctx
    per_group = QUERY_HEADS // KEY_VALUE_HEADS
    sharers = per_group // heads
    head_columns = heads * HEAD_SIZE
    out_columns = MODEL_WIDTH // n_ctx
    score_scale = HEAD_SIZE ** (-0.5)
    gains = [attention_gain, feedforward_gain, query_gain, key_gain]
    small = jnp.concatenate(
        [expert_ids[0].astype(bf16).reshape(-1), route_gates[0].reshape(-1)] + gains
    )
    small = lax.all_gather(small, EVERY, axis=0)
    ids_all = small[:, : rows * TOP].reshape(experts, rows, TOP)
    gates_all = small[:, rows * TOP : 2 * rows * TOP].reshape(experts, rows, TOP)
    at = 2 * rows * TOP
    full_gains = []
    for g in gains:
        width = g.shape[0]
        full_gains.append(small[:n_wa, at : at + width].reshape(-1).astype(f32))
        at += width
    gain_attention, gain_feedforward, gain_query, gain_key = full_gains
    group = my_ctx * heads // per_group
    my_query = lax.dynamic_slice_in_dim(query_weight, my_ctx * head_columns, head_columns, 1)
    my_key = lax.dynamic_slice_in_dim(key_projection_matrix, group * HEAD_SIZE, HEAD_SIZE, 1)
    my_value = lax.dynamic_slice_in_dim(value_projection_matrix, group * HEAD_SIZE, HEAD_SIZE, 1)
    my_out = lax.dynamic_slice_in_dim(output_weight, my_ctx * out_columns, out_columns, 1)
    full_qkv = lax.all_gather(
        jnp.concatenate([my_query, my_key, my_value], axis=1), "wa", axis=0, tiled=True
    )
    full_out = lax.all_gather(my_out, "wa", axis=0, tiled=True)
    out_cotangent = cotangent[0]
    cot_all = lax.all_gather(out_cotangent.astype(bf16), EVERY, axis=0)
    root_x = inv_root(block_rows)
    x_hat = block_rows * root_x
    normed = (x_hat * gain_attention).astype(bf16)
    normed_all = lax.all_gather(normed, "ctx", axis=0, tiled=True)
    cosine, sine = rope_tables(jnp.arange(length, dtype=jnp.int32).astype(f32))
    qkv = dot(normed_all, full_qkv, ((1,), (0,)))
    query = qkv[:, :head_columns].reshape(length, heads, HEAD_SIZE).transpose(1, 0, 2)
    key_raw = qkv[:, head_columns : head_columns + HEAD_SIZE]
    value = qkv[:, head_columns + HEAD_SIZE :].astype(bf16)
    root_q = inv_root(query)
    q_hat = query * root_q
    root_k = inv_root(key_raw)
    k_hat = key_raw * root_k
    q_rot = rotate(q_hat * gain_query, cosine, sine).astype(bf16)
    k_rot = rotate(k_hat * gain_key, cosine, sine).astype(bf16)
    positions = jnp.arange(length, dtype=jnp.int32)
    allowed = positions[:, None] >= positions[None, :]
    scores = jnp.einsum("hqd,kd->hqk", q_rot, k_rot, preferred_element_type=f32) * score_scale
    masked = jnp.where(allowed, scores, VERY_NEGATIVE)
    top = jnp.max(masked, axis=-1, keepdims=True)
    weights = jnp.exp(masked - top)
    total = jnp.sum(weights, axis=-1, keepdims=True)
    attended = (
        jnp.einsum("hqk,kd->hqd", weights.astype(bf16), value, preferred_element_type=f32) / total
    ).astype(bf16)
    lse = top + jnp.log(total)
    attended_rows = attended.transpose(1, 0, 2).reshape(length, head_columns)
    attended_all = lax.all_gather(attended_rows, "ctx", axis=0)
    out_part = jnp.einsum(
        "ctk,ckn->tn",
        attended_all,
        full_out.reshape(n_ctx, head_columns, out_columns),
        preferred_element_type=f32,
    ).astype(bf16)
    out_rows = lax.all_to_all(
        out_part.reshape(n_ctx, rows, out_columns), "ctx", split_axis=0, concat_axis=0, tiled=True
    )
    hidden = block_rows + out_rows.transpose(1, 0, 2).reshape(rows, MODEL_WIDTH).astype(f32)
    root_h = inv_root(hidden)
    h_hat = hidden * root_h
    ffn_in = (h_hat * gain_feedforward).astype(bf16)
    ffn_all = lax.all_gather(ffn_in, EVERY, axis=0)
    me = (my_ctx * n_wa + my_wa).astype(bf16)
    mine = ids_all == me
    hit = jnp.any(mine, axis=-1)
    gate_of = jnp.sum(jnp.where(mine, gates_all.astype(f32), 0.0), axis=-1)
    token = jnp.arange(rows, dtype=jnp.int32)
    before = (token[:, None] < token[None, :]).astype(bf16)
    rank = dot(hit.astype(bf16), before, ((1,), (0,))).astype(jnp.int32)
    slot = jnp.arange(capacity, dtype=jnp.int32)
    chosen = (rank[:, None, :] == slot[None, :, None]) & hit[:, None, :]
    pick = chosen.astype(bf16)
    pick_gate = jnp.where(chosen, gate_of[:, None, :], 0.0).astype(bf16)
    gate_w, up_w, down_w = (expert_gate[0], expert_up[0], expert_down[0])

    def to_slots(one_hot, values):
        return (
            jnp.einsum("bst,btd->bsd", one_hot, values, preferred_element_type=f32)
            .astype(bf16)
            .reshape(experts * capacity, MODEL_WIDTH)
        )

    def to_tokens(one_hot, values):
        return (
            jnp.einsum(
                "bst,bsd->btd",
                one_hot,
                values.reshape(experts, capacity, MODEL_WIDTH),
                preferred_element_type=f32,
            )
            .astype(bf16)
            .reshape(experts * rows, MODEL_WIDTH)
        )

    down_grad = to_slots(pick_gate, cot_all)
    arrived = to_slots(pick, ffn_all)
    gate_pre = dot(arrived, gate_w, ((1,), (0,)))
    up_pre = dot(arrived, up_w, ((1,), (0,)))
    sigmoid_gate = jax.nn.sigmoid(gate_pre)
    activated = gate_pre * sigmoid_gate
    middle = (activated * up_pre).astype(bf16)
    d_middle = dot(down_grad, down_w, ((1,), (1,)))
    d_gate_pre = (
        d_middle * up_pre * sigmoid_gate * (1.0 + gate_pre * (1.0 - sigmoid_gate))
    ).astype(bf16)
    d_up_pre = (d_middle * activated).astype(bf16)
    d_rows = (dot(d_gate_pre, gate_w, ((1,), (1,))) + dot(d_up_pre, up_w, ((1,), (1,)))).astype(
        bf16
    )
    d_ffn = lax.psum_scatter(
        to_tokens(pick, d_rows), EVERY, scatter_dimension=0, tiled=True
    ).astype(f32)
    produced = dot(middle, down_w, ((1,), (0,))).astype(bf16)
    mixture = lax.psum_scatter(
        to_tokens(pick_gate, produced), EVERY, scatter_dimension=0, tiled=True
    ).astype(f32)
    block_output = hidden + mixture
    grad_down = dot(middle, down_grad, ((0,), (0,)))
    grad_gate = dot(arrived, d_gate_pre, ((0,), (0,)))
    grad_up = dot(arrived, d_up_pre, ((0,), (0,)))
    grad_feedforward = jnp.sum(d_ffn * h_hat, axis=0)
    grad_hat = d_ffn * gain_feedforward
    d_hidden = out_cotangent + root_h * (
        grad_hat - h_hat * jnp.mean(grad_hat * h_hat, axis=-1, keepdims=True)
    )
    d_out = lax.all_gather(d_hidden.astype(bf16), "ctx", axis=0, tiled=True)
    out_by_rows = lax.all_to_all(
        full_out.reshape(n_ctx, head_columns, out_columns),
        "ctx",
        split_axis=0,
        concat_axis=0,
        tiled=True,
    )
    d_attended = jnp.einsum(
        "tcn,ckn->tk",
        d_out.reshape(length, n_ctx, out_columns),
        out_by_rows,
        preferred_element_type=f32,
    ).astype(bf16)
    d_attended = d_attended.reshape(length, heads, HEAD_SIZE).transpose(1, 0, 2)
    delta = jnp.sum(d_attended.astype(f32) * attended.astype(f32), axis=-1, keepdims=True)
    scores = jnp.einsum("hqd,kd->hqk", q_rot, k_rot, preferred_element_type=f32) * score_scale
    probs = jnp.where(allowed, jnp.exp(scores - lse), 0.0)
    d_prob = jnp.einsum("hqd,kd->hqk", d_attended, value, preferred_element_type=f32)
    d_round = (probs * (d_prob - delta)).astype(bf16)
    d_value = jnp.einsum("hqk,hqd->kd", probs.astype(bf16), d_attended, preferred_element_type=f32)
    d_krot = jnp.einsum("hqk,hqd->kd", d_round, q_rot, preferred_element_type=f32) * score_scale
    d_qrot = jnp.einsum("hqk,kd->hqd", d_round, k_rot, preferred_element_type=f32) * score_scale
    d_qn = unrotate(d_qrot, cosine, sine)
    d_kn = unrotate(d_krot, cosine, sine)
    grad_qgain = jnp.sum(d_qn * q_hat, axis=(0, 1))
    grad_kgain = jnp.sum(d_kn * k_hat, axis=0)
    grad_q = d_qn * gain_query
    d_query = root_q * (grad_q - q_hat * jnp.mean(grad_q * q_hat, axis=-1, keepdims=True))
    grad_k = d_kn * gain_key
    d_key = root_k * (grad_k - k_hat * jnp.mean(grad_k * k_hat, axis=-1, keepdims=True))
    d_query = d_query.astype(bf16).transpose(1, 0, 2).reshape(length, head_columns)
    d_qkv = jnp.concatenate([d_query, d_key.astype(bf16), d_value.astype(bf16)], axis=1)
    d_normed = lax.psum_scatter(
        dot(d_qkv, full_qkv, ((1,), (1,))).astype(bf16), "ctx", scatter_dimension=0, tiled=True
    ).astype(f32)
    grad_attention = jnp.sum(d_normed * x_hat, axis=0)
    grad_n = d_normed * gain_attention
    input_grad = d_hidden + root_x * (
        grad_n - x_hat * jnp.mean(grad_n * x_hat, axis=-1, keepdims=True)
    )
    my_d_out = lax.dynamic_slice_in_dim(d_out, my_ctx * out_columns, out_columns, 1)
    grad_out = jnp.einsum("ctk,tn->ckn", attended_all, my_d_out, preferred_element_type=f32)
    grad_out = lax.psum_scatter(
        grad_out.astype(bf16).reshape(-1, out_columns), "wa", scatter_dimension=0, tiled=True
    )
    grad_out = lax.all_gather(grad_out, "ctx", axis=0)
    grad_out = grad_out.transpose(1, 0, 2).reshape(-1, MODEL_WIDTH).astype(f32)
    grad_qkv = dot(normed_all, d_qkv, ((0,), (0,))).astype(bf16)
    grad_qkv = lax.psum_scatter(grad_qkv, "wa", scatter_dimension=0, tiled=True)
    grad_qkv = lax.all_gather(grad_qkv, "ctx", axis=0).astype(f32)
    share = grad_qkv.shape[1]
    grad_query = (
        grad_qkv[:, :, :head_columns].transpose(1, 0, 2).reshape(share, QUERY_HEADS * HEAD_SIZE)
    )
    by_group = grad_qkv[:, :, head_columns:].reshape(KEY_VALUE_HEADS, sharers, share, 2, HEAD_SIZE)
    by_group = jnp.sum(by_group, axis=1)
    grad_key = by_group[:, :, 0].transpose(1, 0, 2).reshape(share, KEY_VALUE_HEADS * HEAD_SIZE)
    grad_value = by_group[:, :, 1].transpose(1, 0, 2).reshape(share, KEY_VALUE_HEADS * HEAD_SIZE)
    sums = lax.psum(
        jnp.concatenate([grad_attention, grad_feedforward, grad_qgain, grad_kgain]), EVERY
    )
    gain_grads, at = ([], 0)
    for g in gains:
        width = g.shape[0]
        gain_grads.append(lax.dynamic_slice_in_dim(sums, at + my_wa * width, width, 0))
        at += width * n_wa
    return (
        block_output[None],
        input_grad[None],
        grad_query,
        grad_key,
        grad_value,
        grad_out,
        *gain_grads,
        grad_gate[None],
        grad_up[None],
        grad_down[None],
    )


def solution(mesh):
    by_row, by_expert = (P("wa", None), P(EVERY, None, None))
    tokens = P("wa", "ctx", None)
    gain = P("wa")
    in_specs = (tokens,) + (by_row,) * 4 + (gain,) * 4 + (by_expert,) * 3 + (tokens,) * 3
    out_specs = (tokens,) * 2 + (by_row,) * 4 + (gain,) * 4 + (by_expert,) * 3
    return jax.shard_map(
        on_device, mesh=mesh, in_specs=in_specs, out_specs=out_specs, check_vma=False
    )
```

profile of v0, /device:TPU:0, one launch (start us, length us, event | category | flops | bytes accessed | tf_op | source)
XLA Modules:
  0.0 1365.4 jit_solution(2763674591959409322)
XLA Ops:
  14.5 124.3 %all-reduce.3.cloned.1.call-done = bf16[82944]{0:T(1024)(128)(2,1)} async-done(((bf16[82944]{0:T(1024)(128)(2,1)}), bf16[82944]{0:T(1024)(128)(2,1)}) %all-reduce.3.cloned.1.call-update) | async-done | bytes 165904
  151.3 29.5 %all-gather.13.cloned.1.call-done = bf16[512,2048]{1,0:T(8,128)(2,1)} async-done(((bf16[128,2048]{1,0:T(8,128)(2,1)}), bf16[512,2048]{1,0:T(8,128)(2,1)}) %all-gather.13.cloned.1.call-update) | async-done | bytes 2097168 | tf_op jit(solution)/shard_map/all_gather | solution.py:105
  180.8 58.3 %all-gather.15.cloned.1.call-done = bf16[2048,1280]{1,0:T(8,128)(2,1)} async-done(((bf16[256,1280]{1,0:T(8,128)(2,1)}), bf16[2048,1280]{1,0:T(8,128)(2,1)}) %all-gather.15.cloned.1.call-update) | async-done | bytes 5242896 | tf_op jit(solution)/shard_map/all_gather | solution.py:96
  239.1 6.0 fusion.92
  252.1 3.0 copy.156
  264.6 4.8 fusion.23
  274.1 13.1 all-gather.19.cloned.1.call-done
  287.1 53.7 %all-gather.17.cloned.1.call-done = bf16[4,512,1024]{2,1,0:T(8,128)(2,1)} async-done(((bf16[1,512,1024]{2,1,0:T(8,128)(2,1)}), bf16[4,512,1024]{2,1,0:T(8,128)(2,1)}) %all-gather.17.cloned.1.call-update) | async-done | bytes 4194320 | tf_op jit(solution)/shard_map/all_gather | solution.py:129
  340.8 6.6 fusion.24
  347.4 4.1 all-to-all-start
  351.6 12.0 all-to-all-done
  367.6 2.9 reshape.246
  386.4 75.8 %all-gather.23.cloned.1.call-done = bf16[32,128,2048]{2,1,0:T(8,128)(2,1)} async-done(((bf16[1,128,2048]{2,1,0:T(8,128)(2,1)}), bf16[32,128,2048]{2,1,0:T(8,128)(2,1)}) %all-gather.23.cloned.1.call-update) | async-done | bytes 16777232 | tf_op jit(solution)/shard_map/all_gather | solution.py:101
  462.3 11.4 convolution_convert_fusion.4
  473.7 105.3 %all-gather.21.cloned.1.call-done = bf16[32,128,2048]{2,1,0:T(8,128)(2,1)} async-done(((bf16[1,128,2048]{2,1,0:T(8,128)(2,1)}), bf16[32,128,2048]{2,1,0:T(8,128)(2,1)}) %all-gather.21.cloned.1.call-update) | async-done | bytes 16777232 | tf_op jit(solution)/shard_map/all_gather | solution.py:143
  579.0 11.5 convolution_convert_fusion.5
  590.5 12.0 fusion.14
  602.5 8.5 fusion.18
  611.1 13.9 %multiply_convert_fusion.1 = (bf16[2048,768]{1,0:T(8,128)(2,1)}, bf16[2048,768]{1,0:T(8,128)(2,1)}, bf16[2048,768]{1,0:T(8,128)(2,1)}) fusion(f32[2048,768]{1,0:T(8,128)} %fusion.18, f32[2048,768]{1,0:T(8,128)} %fusion.14, bf16[2048,2048]{1,0:T(8,128)(2,1)S(1)} %bitcast.194, bf16[1,768,2048]{2,1,0:T(8,128)(2,1)S(1)} %copy-done), kind=kOutput, calls=%fused_computation.12 | convolution fusion | flops 6466043904 | bytes 33554432 | tf_op jit(solution)/shard_map/dot_general | solution.py:43
  625.0 12.7 fusion.16
  637.7 12.9 add_convert_fusion
  650.5 13.7 %convolution_convert_fusion = bf16[32,128,2048]{2,1,0:T(8,128)(2,1)} fusion(bf16[32,64,2048]{2,1,0:T(8,128)(2,1)} %bitcast.190, s32[32,128]{1,0:T(8,128)S(1)} %convolution_convert_fusion.8, pred[32,128]{1,0:T(8,128)(4,1)S(1)} %copy.123), kind=kOutput, calls=%fused_computation.1 | convolution fusion | flops 1082654720 | bytes 25186304 | tf_op jit(solution)/shard_map/bst,bsd->btd/dot_general | solution.py:166
  664.3 184.9 %reduce-scatter.8.cloned.1.call-done = bf16[128,2048]{1,0:T(8,128)(2,1)} async-done(((bf16[4096,2048]{1,0:T(8,128)(2,1)}), bf16[128,2048]{1,0:T(8,128)(2,1)}) %reduce-scatter.8.cloned.1.call-update) | async-done | bytes 524304 | tf_op jit(solution)/shard_map/reduce_scatter | solution.py:191
  851.6 2.8 fusion.82
  854.5 4.9 all-to-all-start.1
  859.4 60.8 %all-gather.25.cloned.1.call-done = bf16[512,2048]{1,0:T(8,128)(2,1)} async-done(((bf16[128,2048]{1,0:T(8,128)(2,1)}), bf16[512,2048]{1,0:T(8,128)(2,1)}) %all-gather.25.cloned.1.call-update) | async-done | bytes 2097168 | tf_op jit(solution)/shard_map/all_gather | solution.py:207
  920.2 6.7 convolution_convert_fusion.7
  928.8 4.1 copy.127
  932.9 6.2 bitcast_convert_fusion
  943.8 5.1 multiply_convert_fusion
  956.2 3.3 broadcast_multiply_fusion
  967.1 4.9 convolution_convert_fusion.2
  972.9 7.1 convolution_convert_fusion.6
  980.1 10.9 convolution_convert_fusion.3
  991.0 13.8 %convolution_convert_fusion.1 = bf16[32,128,2048]{2,1,0:T(8,128)(2,1)} fusion(bf16[32,64,2048]{2,1,0:T(8,128)(2,1)} %bitcast.189, bf16[32,128]{1,0:T(8,128)(2,1)S(1)} %copy-done.33, s32[32,128]{1,0:T(8,128)S(1)} %convolution_convert_fusion.8, pred[32,128]{1,0:T(8,128)(4,1)S(1)} %copy-done.29), kind=kOutput, calls=%fused_computation.2 | convolution fusion | flops 1082916864 | bytes 25194496 | tf_op jit(solution)/shard_map/bst,bsd->btd/dot_general | solution.py:166
  1005.5 12.4 convolution_bitcast_fusion.1
  1017.9 20.0 %reduce-scatter.12.cloned.1.call-done = bf16[256,1280]{1,0:T(8,128)(2,1)} async-done(((bf16[2048,1280]{1,0:T(8,128)(2,1)}), bf16[256,1280]{1,0:T(8,128)(2,1)}) %reduce-scatter.12.cloned.1.call-update) | async-done | bytes 655376 | tf_op jit(solution)/shard_map/reduce_scatter | solution.py:256
  1037.9 11.9 convolution_bitcast_fusion
  1049.9 11.2 convolution_bitcast_fusion.2
  1061.0 13.8 %reduce-scatter.10.cloned.1.call-done = bf16[128,2048]{1,0:T(8,128)(2,1)} async-done(((bf16[512,2048]{1,0:T(8,128)(2,1)}), bf16[128,2048]{1,0:T(8,128)(2,1)}) %reduce-scatter.10.cloned.1.call-update) | async-done | bytes 524304 | tf_op jit(solution)/shard_map/reduce_scatter | solution.py:240
  1076.7 41.8 %psum.7 = f32[4352]{0:T(1024)S(1)} all-reduce(f32[4352]{0:T(1024)S(1)} %pad_maximum_fusion.6), channel_id=1, replica_groups=mesh['ctx'=4,'wa'=8] {'ctx','wa'}, use_global_device_ids=true, to_apply=%region_22.23 | all-reduce | flops 4352 | bytes 34816 | tf_op jit(solution)/shard_map/psum | solution.py:266
  1119.7 145.2 %reduce-scatter.6.cloned.1.call-done = bf16[128,2048]{1,0:T(8,128)(2,1)} async-done(((bf16[4096,2048]{1,0:T(8,128)(2,1)}), bf16[128,2048]{1,0:T(8,128)(2,1)}) %reduce-scatter.6.cloned.1.call-update) | async-done | bytes 524304 | tf_op jit(solution)/shard_map/reduce_scatter | solution.py:195
  1265.0 4.1 fusion.39
  1269.0 30.8 %all-gather.29.cloned.1.call-done = bf16[2048,512]{1,0:T(8,128)(2,1)} async-done(((bf16[512,512]{1,0:T(8,128)(2,1)}), bf16[2048,512]{1,0:T(8,128)(2,1)}) %all-gather.29.cloned.1.call-update) | async-done | bytes 2097168 | tf_op jit(solution)/shard_map/all_gather | solution.py:253
  1299.9 3.2 copy.143
  1303.1 4.0 copy.168
  1307.0 34.3 %all-gather.27.cloned.1.call-done = bf16[1024,1280]{1,0:T(8,128)(2,1)} async-done(((bf16[256,1280]{1,0:T(8,128)(2,1)}), bf16[1024,1280]{1,0:T(8,128)(2,1)}) %all-gather.27.cloned.1.call-update) | async-done | bytes 2621456 | tf_op jit(solution)/shard_map/all_gather | solution.py:257
  1343.5 4.5 convert.15
  (269 shorter events, 101.7 us)
Async XLA Ops:
  7.2 603.9 %copy-start = (bf16[1,768,2048]{2,1,0:T(8,128)(2,1)S(1)}, bf16[1,768,2048]{2,1,0:T(8,128)(2,1)}, u32[]{:S(2)}) copy-start(bf16[1,768,2048]{2,1,0:T(8,128)(2,1)} %param.26) | copy-start | bytes 9437188
  7.2 131.5 %all-reduce.3.cloned.1.call-start = ((), (), s32[]{:S(2)}) async-start(), calls=%async_computation.21 | async-start | bytes 331776
  13.0 167.8 %all-gather.13.cloned.1.call-start = ((), (), s32[]{:S(2)}) async-start(), calls=%async_computation.7 | async-start | bytes 2621440 | tf_op jit(solution)/shard_map/all_gather | solution.py:105
  14.4 133.8 %copy-start.55 = (f32[128]{0:T(128)}, f32[128]{0:T(128)S(1)}, u32[]{:S(2)}) copy-start(f32[128]{0:T(128)S(1)} %add_rsqrt_fusion.3) | copy-start | bytes 1540
  139.9 8.3 copy-start.27
  143.3 95.8 %all-gather.15.cloned.1.call-start = ((), (), s32[]{:S(2)}) async-start(), calls=%async_computation.8 | async-start | bytes 5898240 | tf_op jit(solution)/shard_map/all_gather | solution.py:96
  146.3 140.8 %all-gather.19.cloned.1.call-start = ((), (), s32[]{:S(2)}) async-start(), calls=%async_computation.10 | async-start | bytes 4718592 | tf_op jit(solution)/shard_map/all_gather | solution.py:99
  148.3 192.5 %all-gather.17.cloned.1.call-start = ((), (), s32[]{:S(2)}) async-start(), calls=%async_computation.9 | async-start | bytes 5242880 | tf_op jit(solution)/shard_map/all_gather | solution.py:129
  151.2 106.9 %copy-start.51 = (f32[128]{0:T(128)}, f32[128]{0:T(128)S(1)}, u32[]{:S(2)}) copy-start(f32[128]{0:T(128)S(1)} %reshape.242) | copy-start | bytes 1540
  151.3 95.9 %copy-start.49 = (f32[128]{0:T(128)}, f32[128]{0:T(128)S(1)}, u32[]{:S(2)}) copy-start(f32[128]{0:T(128)S(1)} %reshape.243) | copy-start | bytes 1540
  248.5 11.2 copy-start.19
  263.0 6.4 copy-start.36
  271.7 190.5 %all-gather.23.cloned.1.call-start = ((), (), s32[]{:S(2)}) async-start(), calls=%async_computation.13 | async-start | bytes 17301504 | tf_op jit(solution)/shard_map/all_gather | solution.py:101
  340.8 10.8 copy-start.46
  347.4 16.2 %all-to-all-start = ((bf16[4,128,512]{2,1,0:T(8,128)(2,1)}), bf16[4,128,512]{2,1,0:T(8,128)(2,1)}, u32[]{:S(2)}, u32[]{:S(2)}) async-start(bf16[4,128,512]{2,1,0:T(8,128)(2,1)} %bitcast.219), calls=%async_computation | async-start | bytes 1048576 | tf_op jit(solution)/shard_map/all_to_all | solution.py:136
  351.5 227.4 %all-gather.21.cloned.1.call-start = ((), (), s32[]{:S(2)}) async-start(), calls=%async_computation.11 | async-start | bytes 17301504 | tf_op jit(solution)/shard_map/all_gather | solution.py:143
  351.6 500.0 %copy-start.34 = (f32[1,2,8,128]{3,1,2,0:T(2,128)}, f32[1,2,8,128]{3,1,2,0:T(2,128)S(1)}, u32[]{:S(2)}) copy-start(f32[1,2,8,128]{3,1,2,0:T(2,128)S(1)} %copy.165) | copy-start | bytes 24580
  374.3 477.4 %copy-start.53 = (f32[128]{0:T(128)}, f32[128]{0:T(128)S(1)}, u32[]{:S(2)}) copy-start(f32[128]{0:T(128)S(1)} %add_rsqrt_fusion.2) | copy-start | bytes 1540
  375.3 474.0 %reduce-scatter.8.cloned.1.call-start = ((), (), s32[]{:S(2)}) async-start(), calls=%async_computation.14 | async-start | bytes 17301504 | tf_op jit(solution)/shard_map/reduce_scatter | solution.py:191
  379.4 271.1 %copy-start.28 = (pred[32,128]{1,0:T(8,128)(4,1)}, pred[32,128]{1,0:T(8,128)(4,1)S(1)}, u32[]{:S(2)}) copy-start(pred[32,128]{1,0:T(8,128)(4,1)S(1)} %copy.123) | copy-start | bytes 12292
  385.5 88.2 %copy-start.32 = (bf16[32,128]{1,0:T(8,128)(2,1)}, bf16[32,128]{1,0:T(8,128)(2,1)S(1)}, u32[]{:S(2)}) copy-start(bf16[32,128]{1,0:T(8,128)(2,1)S(1)} %copy.125) | copy-start | bytes 24580
  579.0 11.5 copy-start.62
  590.5 12.0 copy-start.5
  590.5 12.0 copy-start.61
  590.5 20.6 %slice-start.2 = ((s8[8388608]{0:T(1024)(128)(4,1)}), s8[4194304]{0:T(1024)(128)(4,1)S(1)}, s32[]{:S(2)}) async-start(s8[8388608]{0:T(1024)(128)(4,1)} %bitcast.192), calls=%async_computation.24 | async-start | bytes 8388608
  602.5 8.5 slice-start.3
  625.0 12.7 copy-start.63
  625.0 12.7 copy-start.66
  664.3 255.9 %all-gather.25.cloned.1.call-start = ((), (), s32[]{:S(2)}) async-start(), calls=%async_computation.15 | async-start | bytes 2621440 | tf_op jit(solution)/shard_map/all_gather | solution.py:207
  854.5 78.4 %all-to-all-start.1 = ((bf16[4,1024,512]{2,1,0:T(8,128)(2,1)}), bf16[4,1024,512]{2,1,0:T(8,128)(2,1)}, u32[]{:S(2)}, u32[]{:S(2)}) async-start(bf16[4,1024,512]{2,1,0:T(8,128)(2,1)} %bitcast.205), calls=%async_computation.3 | async-start | bytes 8388608 | tf_op jit(solution)/shard_map/all_to_all | solution.py:208
  859.4 145.6 %reduce-scatter.14.cloned.1.call-start = ((), (), s32[]{:S(2)}) async-start(), calls=%async_computation.18 | async-start | bytes 4718592 | tf_op jit(solution)/shard_map/reduce_scatter | solution.py:250
  926.9 110.9 %reduce-scatter.12.cloned.1.call-start = ((), (), s32[]{:S(2)}) async-start(), calls=%async_computation.17 | async-start | bytes 5898240 | tf_op jit(solution)/shard_map/reduce_scatter | solution.py:256
  928.8 14.9 %copy-start.47 = (f32[8,512]{1,0:T(8,128)}, f32[8,512]{1,0:T(8,128)S(1)}, u32[]{:S(2)}) copy-start(f32[8,512]{1,0:T(8,128)S(1)} %log_add_fusion) | copy-start | bytes 49156
  972.0 102.8 %reduce-scatter.10.cloned.1.call-start = ((), (), s32[]{:S(2)}) async-start(), calls=%async_computation.16 | async-start | bytes 2621440 | tf_op jit(solution)/shard_map/reduce_scatter | solution.py:240
  980.1 284.9 %reduce-scatter.6.cloned.1.call-start = ((), (), s32[]{:S(2)}) async-start(), calls=%async_computation.12 | async-start | bytes 17301504 | tf_op jit(solution)/shard_map/reduce_scatter | solution.py:195
  980.1 10.9 copy-start.29
  980.1 10.9 copy-start.33
  1004.9 295.0 %all-gather.29.cloned.1.call-start = ((), (), s32[]{:S(2)}) async-start(), calls=%async_computation.20 | async-start | bytes 2621440 | tf_op jit(solution)/shard_map/all_gather | solution.py:253
  1005.5 335.9 %all-gather.27.cloned.1.call-start = ((), (), s32[]{:S(2)}) async-start(), calls=%async_computation.19 | async-start | bytes 3276800 | tf_op jit(solution)/shard_map/all_gather | solution.py:257
  1037.9 11.9 copy-start.65
  1049.8 25.0 %copy-start.41 = (f32[1,2,8,128]{3,1,2,0:T(2,128)S(1)}, f32[1,2,8,128]{3,1,2,0:T(2,128)}, u32[]{:S(2)}) copy-start(f32[1,2,8,128]{3,1,2,0:T(2,128)} %copy-done.40) | copy-start | bytes 24580
  1049.8 25.0 %copy-start.56 = (f32[128]{0:T(128)S(1)}, f32[128]{0:T(128)}, u32[]{:S(2)}) copy-start(f32[128]{0:T(128)} %copy-done.55) | copy-start | bytes 1540
  1049.8 26.8 %copy-start.45 = (f32[2048]{0:T(1024)S(1)}, f32[2048]{0:T(1024)}, u32[]{:S(2)}) copy-start(f32[2048]{0:T(1024)} %get-tuple-element.19) | copy-start | bytes 24580
  1049.8 26.8 %copy-start.59 = (f32[128]{0:T(128)S(1)}, f32[128]{0:T(128)}, u32[]{:S(2)}) copy-start(f32[128]{0:T(128)} %get-tuple-element.13) | copy-start | bytes 1540
  1049.8 26.8 %copy-start.60 = (f32[128]{0:T(128)S(1)}, f32[128]{0:T(128)}, u32[]{:S(2)}) copy-start(f32[128]{0:T(128)} %get-tuple-element.15) | copy-start | bytes 1540
  1049.8 215.1 %copy-start.35 = (f32[1,2,8,128]{3,1,2,0:T(2,128)S(1)}, f32[1,2,8,128]{3,1,2,0:T(2,128)}, u32[]{:S(2)}) copy-start(f32[1,2,8,128]{3,1,2,0:T(2,128)} %copy-done.34) | copy-start | bytes 24580
  1049.9 215.1 %copy-start.54 = (f32[128]{0:T(128)S(1)}, f32[128]{0:T(128)}, u32[]{:S(2)}) copy-start(f32[128]{0:T(128)} %copy-done.53) | copy-start | bytes 1540
  1049.9 215.1 %copy-start.58 = (f32[128]{0:T(128)S(1)}, f32[128]{0:T(128)}, u32[]{:S(2)}) copy-start(f32[128]{0:T(128)} %copy-done.57) | copy-start | bytes 1540
  (42 other events, 95.1 us)
Sparse Core Ops, SparseCore 0:
  14.1 124.5 all-reduce.2
  143.5 37.2 all-gather.12
  183.0 56.0 all-gather.14
  241.1 45.9 all-gather.18
  289.4 51.3 all-gather.16
  344.2 117.9 all-gather.22
  465.8 113.0 all-gather.20
  664.4 184.7 reduce-scatter.7
  854.6 65.5 all-gather.24
  927.0 49.7 reduce-scatter.13
  979.8 58.0 reduce-scatter.11
  1041.2 33.5 reduce-scatter.9
  1077.2 187.6 reduce-scatter.5
  1266.8 33.0 all-gather.28
  1301.7 39.6 all-gather.26
where the time goes:
time: 1380 us; the launch traced here: 1370 us
  waiting for transfers between devices  962 us (70%)
  matrix products  213 us (15%)
  local copies, waits for them, and re-layouts  70.5 us (5%)
  other arithmetic  52.6 us (4%)
  blocking collectives  41.8 us (3%)
  between operations  15 us (1%)
    reduce_scatter x1, waiting for transfers between devices, on_device(): lax.psum_scatter(to_tokens(pick, d_rows), EVERY, scatter_dimension=0, til...  185 us
    reduce_scatter x1, waiting for transfers between devices, on_device(): lax.psum_scatter(to_tokens(pick_gate, produced), EVERY, scatter_dimension...  145 us
    dot_general x13, matrix products, dot(): lax.dot_general(a, b, (contract, ((), ())), preferred_element_type=jnp.fl...  125 us
    unnamed x16, waiting for transfers between devices  125 us
    all_gather x1, waiting for transfers between devices, on_device(): ffn_all = lax.all_gather(ffn_in, EVERY, axis=0)  105 us
    all_gather x1, waiting for transfers between devices, on_device(): cot_all = lax.all_gather(out_cotangent.astype(bf16), EVERY, axis=0)  75.8 us
    all_gather x1, waiting for transfers between devices, on_device(): d_out = lax.all_gather(d_hidden.astype(bf16), 'ctx', axis=0, tiled=True)  60.8 us
    all_gather x1, waiting for transfers between devices, on_device(): lax.all_gather(jnp.concatenate([my_query, my_key, my_value], axis=1), 'wa...  58.3 us
  transfers between devices with their start and end apart: 17, of which 15 were waited for; matrix products, arithmetic and copies ran while one was open for 15% of the time, Pallas kernels for 0%

commit v1 on v0

--- a/solution.py
+++ b/solution.py
@@ -102,7 +102,12 @@
     root_x = inv_root(block_rows)
     x_hat = block_rows * root_x
     normed = (x_hat * gain_attention).astype(bf16)
-    normed_all = lax.all_gather(normed, "ctx", axis=0, tiled=True)
+    ring = [normed]
+    for hop in range(3):
+        ring.append(lax.ppermute(ring[-1], "ctx", [(dev, (dev + 1) % 4) for dev in range(4)]))
+    normed_all = jnp.roll(
+        jnp.concatenate(ring[::-1], axis=0), (lax.axis_index("ctx") + 1) * ring[0].shape[0], axis=0
+    )
     cosine, sine = rope_tables(jnp.arange(length, dtype=jnp.int32).astype(f32))
     qkv = dot(normed_all, full_qkv, ((1,), (0,)))
     query = qkv[:, :head_columns].reshape(length, heads, HEAD_SIZE).transpose(1, 0, 2)

time: 1380 us -> 1360 us (0.986)
  waiting for transfers between devices: 962 us -> 920 us
    all_gather x1, waiting for transfers between devices: 58.3 us -> 0.01 us  [on_device(): lax.all_gather(jnp.concatenate([my_query, my_key, my_value], axis=1), 'wa...]
    ppermute x0 -> x3, waiting for transfers between devices: none -> 36.5 us  [on_device(): lax.ppermute(ring[-1], 'ctx', [(dev, (dev + 1) % 4) for dev in range(4)])]
    unnamed x16 -> x15, waiting for transfers between devices: 125 us -> 157 us
    all_gather x1 -> x0, waiting for transfers between devices: 29.5 us -> none  [on_device(): normed_all = lax.all_gather(normed, 'ctx', axis=0, tiled=True)]
  transfers between devices with their start and end apart: 17 -> 19, of which waited for: 15 -> 15; matrix products, arithmetic and copies ran while one was open for 15% -> 17% of each run, Pallas kernels for 0% -> 0%
where the time goes in v1:
time: 1360 us; the launch traced here: 1340 us
  waiting for transfers between devices  920 us (68%)
  matrix products  216 us (16%)
  local copies, waits for them, and re-layouts  79.4 us (6%)
  other arithmetic  56.6 us (4%)
  blocking collectives  42 us (3%)
  between operations  17.1 us (1%)
    reduce_scatter x1, waiting for transfers between devices, on_device(): lax.psum_scatter(to_tokens(pick, d_rows), EVERY, scatter_dimension=0, til...  185 us
    unnamed x15, waiting for transfers between devices  157 us
    reduce_scatter x1, waiting for transfers between devices, on_device(): lax.psum_scatter(to_tokens(pick_gate, produced), EVERY, scatter_dimension...  145 us
    dot_general x13, matrix products, dot(): lax.dot_general(a, b, (contract, ((), ())), preferred_element_type=jnp.fl...  127 us
    all_gather x1, waiting for transfers between devices, on_device(): ffn_all = lax.all_gather(ffn_in, EVERY, axis=0)  105 us
    all_gather x1, waiting for transfers between devices, on_device(): cot_all = lax.all_gather(out_cotangent.astype(bf16), EVERY, axis=0)  75.5 us
    all_gather x1, waiting for transfers between devices, on_device(): d_out = lax.all_gather(d_hidden.astype(bf16), 'ctx', axis=0, tiled=True)  60.7 us
    all_gather x1, waiting for transfers between devices, on_device(): attended_all = lax.all_gather(attended_rows, 'ctx', axis=0)  48 us
  transfers between devices with their start and end apart: 19, of which 15 were waited for; matrix products, arithmetic and copies ran while one was open for 17% of the time, Pallas kernels for 0%

profile of v1, /device:TPU:0, one launch (start us, length us, event | category | flops | bytes accessed | tf_op | source)
XLA Modules:
  0.0 1344.1 jit_solution(8932586800063248973)
XLA Ops:
  18.3 156.8 %all-reduce.3.cloned.1.call-done = bf16[82944]{0:T(1024)(128)(2,1)} async-done(((bf16[82944]{0:T(1024)(128)(2,1)}), bf16[82944]{0:T(1024)(128)(2,1)}) %all-reduce.3.cloned.1.call-update) | async-done | bytes 165904
  179.8 13.7 %collective-permute-done = bf16[128,2048]{1,0:T(8,128)(2,1)} collective-permute-done((bf16[128,2048]{1,0:T(8,128)(2,1)S(1)}, bf16[128,2048]{1,0:T(8,128)(2,1)}, u32[]{:S(2)}, u32[]{:S(2)}) %collective-permute-start) | collective-permute-done | bytes 524320 | tf_op jit(solution)/shard_map/ppermute | solution.py:107
  196.2 12.0 collective-permute-done.1
  211.0 10.8 collective-permute-done.2
  236.3 6.0 fusion.25
  249.3 2.9 copy.156
  262.2 4.8 fusion.23
  271.7 48.0 %all-gather.14.cloned.1.call-done = bf16[4,512,1024]{2,1,0:T(8,128)(2,1)} async-done(((bf16[1,512,1024]{2,1,0:T(8,128)(2,1)}), bf16[4,512,1024]{2,1,0:T(8,128)(2,1)}) %all-gather.14.cloned.1.call-update) | async-done | bytes 4194320 | tf_op jit(solution)/shard_map/all_gather | solution.py:134
  319.7 6.6 fusion.27
  326.3 4.1 all-to-all-start
  330.5 11.9 all-to-all-done
  346.4 2.9 reshape.246
  365.3 75.5 %all-gather.20.cloned.1.call-done = bf16[32,128,2048]{2,1,0:T(8,128)(2,1)} async-done(((bf16[1,128,2048]{2,1,0:T(8,128)(2,1)}), bf16[32,128,2048]{2,1,0:T(8,128)(2,1)}) %all-gather.20.cloned.1.call-update) | async-done | bytes 16777232 | tf_op jit(solution)/shard_map/all_gather | solution.py:101
  440.8 11.4 convolution_convert_fusion.4
  452.2 105.2 %all-gather.18.cloned.1.call-done = bf16[32,128,2048]{2,1,0:T(8,128)(2,1)} async-done(((bf16[1,128,2048]{2,1,0:T(8,128)(2,1)}), bf16[32,128,2048]{2,1,0:T(8,128)(2,1)}) %all-gather.18.cloned.1.call-update) | async-done | bytes 16777232 | tf_op jit(solution)/shard_map/all_gather | solution.py:148
  557.4 11.5 convolution_convert_fusion.5
  568.9 12.2 fusion.14
  581.1 8.5 fusion.18
  589.6 13.9 %multiply_convert_fusion.1 = (bf16[2048,768]{1,0:T(8,128)(2,1)}, bf16[2048,768]{1,0:T(8,128)(2,1)}, bf16[2048,768]{1,0:T(8,128)(2,1)}) fusion(f32[2048,768]{1,0:T(8,128)} %fusion.18, f32[2048,768]{1,0:T(8,128)} %fusion.14, bf16[2048,2048]{1,0:T(8,128)(2,1)S(1)} %bitcast.196, bf16[1,768,2048]{2,1,0:T(8,128)(2,1)S(1)} %copy-done), kind=kOutput, calls=%fused_computation.12 | convolution fusion | flops 6466043904 | bytes 33554432 | tf_op jit(solution)/shard_map/dot_general | solution.py:43
  603.5 12.8 fusion.16
  616.4 12.6 add_convert_fusion
  628.9 13.7 %convolution_convert_fusion = bf16[32,128,2048]{2,1,0:T(8,128)(2,1)} fusion(bf16[32,64,2048]{2,1,0:T(8,128)(2,1)} %bitcast.192, s32[32,128]{1,0:T(8,128)S(1)} %convolution_convert_fusion.8, pred[32,128]{1,0:T(8,128)(4,1)S(1)} %copy.123), kind=kOutput, calls=%fused_computation.1 | convolution fusion | flops 1082654720 | bytes 25186304 | tf_op jit(solution)/shard_map/bst,bsd->btd/dot_general | solution.py:171
  642.7 184.9 %reduce-scatter.8.cloned.1.call-done = bf16[128,2048]{1,0:T(8,128)(2,1)} async-done(((bf16[4096,2048]{1,0:T(8,128)(2,1)}), bf16[128,2048]{1,0:T(8,128)(2,1)}) %reduce-scatter.8.cloned.1.call-update) | async-done | bytes 524304 | tf_op jit(solution)/shard_map/reduce_scatter | solution.py:196
  830.1 2.8 fusion.87
  832.9 4.9 all-to-all-start.1
  837.8 60.7 %all-gather.22.cloned.1.call-done = bf16[512,2048]{1,0:T(8,128)(2,1)} async-done(((bf16[128,2048]{1,0:T(8,128)(2,1)}), bf16[512,2048]{1,0:T(8,128)(2,1)}) %all-gather.22.cloned.1.call-update) | async-done | bytes 2097168 | tf_op jit(solution)/shard_map/all_gather | solution.py:212
  898.6 6.7 convolution_convert_fusion.7
  907.2 3.9 copy.127
  911.1 6.2 bitcast_convert_fusion
  922.3 6.7 multiply_convert_fusion
  936.0 3.3 broadcast_multiply_fusion
  946.9 6.9 convolution_convert_fusion.2
  954.8 7.1 convolution_convert_fusion.6
  961.9 10.9 convolution_convert_fusion.3
  972.9 13.8 %convolution_convert_fusion.1 = bf16[32,128,2048]{2,1,0:T(8,128)(2,1)} fusion(bf16[32,64,2048]{2,1,0:T(8,128)(2,1)} %bitcast.191, bf16[32,128]{1,0:T(8,128)(2,1)S(1)} %copy-done.35, s32[32,128]{1,0:T(8,128)S(1)} %convolution_convert_fusion.8, pred[32,128]{1,0:T(8,128)(4,1)S(1)} %copy-done.29), kind=kOutput, calls=%fused_computation.2 | convolution fusion | flops 1082916864 | bytes 25194496 | tf_op jit(solution)/shard_map/bst,bsd->btd/dot_general | solution.py:171
  987.6 12.0 convolution_bitcast_fusion.1
  999.6 16.2 %reduce-scatter.12.cloned.1.call-done = bf16[256,1280]{1,0:T(8,128)(2,1)} async-done(((bf16[2048,1280]{1,0:T(8,128)(2,1)}), bf16[256,1280]{1,0:T(8,128)(2,1)}) %reduce-scatter.12.cloned.1.call-update) | async-done | bytes 655376 | tf_op jit(solution)/shard_map/reduce_scatter | solution.py:261
  1015.8 11.9 convolution_bitcast_fusion
  1027.8 11.2 convolution_bitcast_fusion.2
  1039.0 13.7 %reduce-scatter.10.cloned.1.call-done = bf16[128,2048]{1,0:T(8,128)(2,1)} async-done(((bf16[512,2048]{1,0:T(8,128)(2,1)}), bf16[128,2048]{1,0:T(8,128)(2,1)}) %reduce-scatter.10.cloned.1.call-update) | async-done | bytes 524304 | tf_op jit(solution)/shard_map/reduce_scatter | solution.py:245
  1054.5 42.0 %psum.7 = f32[4352]{0:T(1024)S(1)} all-reduce(f32[4352]{0:T(1024)S(1)} %pad_maximum_fusion.6), channel_id=1, replica_groups=mesh['ctx'=4,'wa'=8] {'ctx','wa'}, use_global_device_ids=true, to_apply=%region_22.23 | all-reduce | flops 4352 | bytes 34816 | tf_op jit(solution)/shard_map/psum | solution.py:271
  1097.8 144.9 %reduce-scatter.6.cloned.1.call-done = bf16[128,2048]{1,0:T(8,128)(2,1)} async-done(((bf16[4096,2048]{1,0:T(8,128)(2,1)}), bf16[128,2048]{1,0:T(8,128)(2,1)}) %reduce-scatter.6.cloned.1.call-update) | async-done | bytes 524304 | tf_op jit(solution)/shard_map/reduce_scatter | solution.py:200
  1242.7 4.1 fusion.42
  1246.7 30.6 %all-gather.26.cloned.1.call-done = bf16[2048,512]{1,0:T(8,128)(2,1)} async-done(((bf16[512,512]{1,0:T(8,128)(2,1)}), bf16[2048,512]{1,0:T(8,128)(2,1)}) %all-gather.26.cloned.1.call-update) | async-done | bytes 2097168 | tf_op jit(solution)/shard_map/all_gather | solution.py:258
  1277.4 3.2 copy.143
  1280.6 4.0 copy.168
  1284.5 34.3 %all-gather.24.cloned.1.call-done = bf16[1024,1280]{1,0:T(8,128)(2,1)} async-done(((bf16[256,1280]{1,0:T(8,128)(2,1)}), bf16[1024,1280]{1,0:T(8,128)(2,1)}) %all-gather.24.cloned.1.call-update) | async-done | bytes 2621456 | tf_op jit(solution)/shard_map/all_gather | solution.py:262
  1321.0 4.5 convert.15
  (278 shorter events, 117.4 us)
Async XLA Ops:
  8.0 581.6 %copy-start = (bf16[1,768,2048]{2,1,0:T(8,128)(2,1)S(1)}, bf16[1,768,2048]{2,1,0:T(8,128)(2,1)}, u32[]{:S(2)}) copy-start(bf16[1,768,2048]{2,1,0:T(8,128)(2,1)} %param.26) | copy-start | bytes 9437188
  8.0 167.0 %all-reduce.3.cloned.1.call-start = ((), (), s32[]{:S(2)}) async-start(), calls=%async_computation.20 | async-start | bytes 331776
  13.8 222.4 %all-gather.12.cloned.1.call-start = ((), (), s32[]{:S(2)}) async-start(), calls=%async_computation.7 | async-start | bytes 5898240 | tf_op jit(solution)/shard_map/all_gather | solution.py:96
  16.8 254.9 %all-gather.16.cloned.1.call-start = ((), (), s32[]{:S(2)}) async-start(), calls=%async_computation.9 | async-start | bytes 4718592 | tf_op jit(solution)/shard_map/all_gather | solution.py:99
  18.2 217.0 %copy-start.49 = (f32[128]{0:T(128)}, f32[128]{0:T(128)S(1)}, u32[]{:S(2)}) copy-start(f32[128]{0:T(128)S(1)} %add_rsqrt_fusion.3) | copy-start | bytes 1540
  176.2 19.9 %copy-start.27 = (bf16[32,2592]{1,0:T(8,128)(2,1)}, bf16[32,2592]{1,0:T(8,128)(2,1)S(1)}, u32[]{:S(2)}) copy-start(bf16[32,2592]{1,0:T(8,128)(2,1)S(1)} %reshape.249) | copy-start | bytes 497668
  176.9 58.4 %copy-start.32 = (f32[1,2,8,128]{3,1,2,0:T(2,128)}, f32[1,2,8,128]{3,1,2,0:T(2,128)S(1)}, u32[]{:S(2)}) copy-start(f32[1,2,8,128]{3,1,2,0:T(2,128)S(1)} %copy.164) | copy-start | bytes 24580
  178.3 15.3 %collective-permute-start = (bf16[128,2048]{1,0:T(8,128)(2,1)S(1)}, bf16[128,2048]{1,0:T(8,128)(2,1)}, u32[]{:S(2)}, u32[]{:S(2)}) collective-permute-start(bf16[128,2048]{1,0:T(8,128)(2,1)S(1)} %multiply_convert_fusion.6), channel_id=1, source_target_pairs={{0,8},{8,16},{16,24},{24,0},{1,9},{9,17},{17,25},{25,1},{2,10},{10... | collective-permute-start | bytes 1572872 | tf_op jit(solution)/shard_map/ppermute | solution.py:107
  193.5 14.6 %collective-permute-start.1 = (bf16[128,2048]{1,0:T(8,128)(2,1)}, bf16[128,2048]{1,0:T(8,128)(2,1)}, u32[]{:S(2)}, u32[]{:S(2)}) collective-permute-start(bf16[128,2048]{1,0:T(8,128)(2,1)} %collective-permute-done), channel_id=1, source_target_pairs={{0,8},{8,16},{16,24},{24,0},{1,9},{9,17},{17,25},{25,1},{2,10},{10... | collective-permute-start | bytes 1572872 | tf_op jit(solution)/shard_map/ppermute | solution.py:107
  196.0 123.7 %all-gather.14.cloned.1.call-start = ((), (), s32[]{:S(2)}) async-start(), calls=%async_computation.8 | async-start | bytes 5242880 | tf_op jit(solution)/shard_map/all_gather | solution.py:134
  208.1 13.7 %collective-permute-start.2 = (bf16[128,2048]{1,0:T(8,128)(2,1)}, bf16[128,2048]{1,0:T(8,128)(2,1)}, u32[]{:S(2)}, u32[]{:S(2)}) collective-permute-start(bf16[128,2048]{1,0:T(8,128)(2,1)} %collective-permute-done.1), channel_id=1, source_target_pairs={{0,8},{8,16},{16,24},{24,0},{1,9},{9,17},{17,25},{25,1},{2,10},{10... | collective-permute-start | bytes 1572872 | tf_op jit(solution)/shard_map/ppermute | solution.py:107
  210.9 45.6 %copy-start.53 = (f32[128]{0:T(128)}, f32[128]{0:T(128)S(1)}, u32[]{:S(2)}) copy-start(f32[128]{0:T(128)S(1)} %reshape.242) | copy-start | bytes 1540
  211.0 33.4 %copy-start.51 = (f32[128]{0:T(128)}, f32[128]{0:T(128)S(1)}, u32[]{:S(2)}) copy-start(f32[128]{0:T(128)S(1)} %reshape.243) | copy-start | bytes 1540
  211.0 24.3 %copy-start.3 = (f32[1,128,2048]{2,1,0:T(8,128)S(1)}, f32[1,128,2048]{2,1,0:T(8,128)}, u32[]{:S(2)}) copy-start(f32[1,128,2048]{2,1,0:T(8,128)} %param.15) | copy-start | bytes 3145732
  245.7 11.7 copy-start.19
  269.3 171.5 %all-gather.20.cloned.1.call-start = ((), (), s32[]{:S(2)}) async-start(), calls=%async_computation.12 | async-start | bytes 17301504 | tf_op jit(solution)/shard_map/all_gather | solution.py:101
  326.3 16.2 %all-to-all-start = ((bf16[4,128,512]{2,1,0:T(8,128)(2,1)}), bf16[4,128,512]{2,1,0:T(8,128)(2,1)}, u32[]{:S(2)}, u32[]{:S(2)}) async-start(bf16[4,128,512]{2,1,0:T(8,128)(2,1)} %bitcast.221), calls=%async_computation | async-start | bytes 1048576 | tf_op jit(solution)/shard_map/all_to_all | solution.py:141
  330.4 226.9 %all-gather.18.cloned.1.call-start = ((), (), s32[]{:S(2)}) async-start(), calls=%async_computation.10 | async-start | bytes 17301504 | tf_op jit(solution)/shard_map/all_gather | solution.py:148
  330.5 499.5 %copy-start.36 = (f32[1,2,8,128]{3,1,2,0:T(2,128)}, f32[1,2,8,128]{3,1,2,0:T(2,128)S(1)}, u32[]{:S(2)}) copy-start(f32[1,2,8,128]{3,1,2,0:T(2,128)S(1)} %copy.165) | copy-start | bytes 24580
  353.1 477.0 %copy-start.55 = (f32[128]{0:T(128)}, f32[128]{0:T(128)S(1)}, u32[]{:S(2)}) copy-start(f32[128]{0:T(128)S(1)} %add_rsqrt_fusion.2) | copy-start | bytes 1540
  354.1 473.6 %reduce-scatter.8.cloned.1.call-start = ((), (), s32[]{:S(2)}) async-start(), calls=%async_computation.13 | async-start | bytes 17301504 | tf_op jit(solution)/shard_map/reduce_scatter | solution.py:196
  358.2 270.7 %copy-start.28 = (pred[32,128]{1,0:T(8,128)(4,1)}, pred[32,128]{1,0:T(8,128)(4,1)S(1)}, u32[]{:S(2)}) copy-start(pred[32,128]{1,0:T(8,128)(4,1)S(1)} %copy.123) | copy-start | bytes 12292
  364.3 87.9 %copy-start.34 = (bf16[32,128]{1,0:T(8,128)(2,1)}, bf16[32,128]{1,0:T(8,128)(2,1)S(1)}, u32[]{:S(2)}) copy-start(bf16[32,128]{1,0:T(8,128)(2,1)S(1)} %copy.125) | copy-start | bytes 24580
  557.4 11.5 copy-start.62
  568.9 12.2 copy-start.6
  568.9 12.2 copy-start.61
  568.9 20.7 %slice-start.2 = ((s8[8388608]{0:T(1024)(128)(4,1)}), s8[4194304]{0:T(1024)(128)(4,1)S(1)}, s32[]{:S(2)}) async-start(s8[8388608]{0:T(1024)(128)(4,1)} %bitcast.194), calls=%async_computation.23 | async-start | bytes 8388608
  603.5 12.8 copy-start.63
  603.5 12.8 copy-start.65
  642.7 255.9 %all-gather.22.cloned.1.call-start = ((), (), s32[]{:S(2)}) async-start(), calls=%async_computation.14 | async-start | bytes 2621440 | tf_op jit(solution)/shard_map/all_gather | solution.py:212
  832.9 78.2 %all-to-all-start.1 = ((bf16[4,1024,512]{2,1,0:T(8,128)(2,1)}), bf16[4,1024,512]{2,1,0:T(8,128)(2,1)}, u32[]{:S(2)}, u32[]{:S(2)}) async-start(bf16[4,1024,512]{2,1,0:T(8,128)(2,1)} %bitcast.207), calls=%async_computation.3 | async-start | bytes 8388608 | tf_op jit(solution)/shard_map/all_to_all | solution.py:213
  837.8 149.0 %reduce-scatter.14.cloned.1.call-start = ((), (), s32[]{:S(2)}) async-start(), calls=%async_computation.17 | async-start | bytes 4718592 | tf_op jit(solution)/shard_map/reduce_scatter | solution.py:255
  905.3 110.5 %reduce-scatter.12.cloned.1.call-start = ((), (), s32[]{:S(2)}) async-start(), calls=%async_computation.16 | async-start | bytes 5898240 | tf_op jit(solution)/shard_map/reduce_scatter | solution.py:261
  907.2 15.1 %copy-start.47 = (f32[8,512]{1,0:T(8,128)}, f32[8,512]{1,0:T(8,128)S(1)}, u32[]{:S(2)}) copy-start(f32[8,512]{1,0:T(8,128)S(1)} %log_add_fusion) | copy-start | bytes 49156
  953.9 98.8 %reduce-scatter.10.cloned.1.call-start = ((), (), s32[]{:S(2)}) async-start(), calls=%async_computation.15 | async-start | bytes 2621440 | tf_op jit(solution)/shard_map/reduce_scatter | solution.py:245
  961.9 280.8 %reduce-scatter.6.cloned.1.call-start = ((), (), s32[]{:S(2)}) async-start(), calls=%async_computation.11 | async-start | bytes 17301504 | tf_op jit(solution)/shard_map/reduce_scatter | solution.py:200
  961.9 11.0 copy-start.29
  986.8 290.6 %all-gather.26.cloned.1.call-start = ((), (), s32[]{:S(2)}) async-start(), calls=%async_computation.19 | async-start | bytes 2621440 | tf_op jit(solution)/shard_map/all_gather | solution.py:258
  987.3 331.5 %all-gather.24.cloned.1.call-start = ((), (), s32[]{:S(2)}) async-start(), calls=%async_computation.18 | async-start | bytes 3276800 | tf_op jit(solution)/shard_map/all_gather | solution.py:262
  1015.8 11.9 copy-start.64
  1027.8 25.0 %copy-start.33 = (f32[1,2,8,128]{3,1,2,0:T(2,128)S(1)}, f32[1,2,8,128]{3,1,2,0:T(2,128)}, u32[]{:S(2)}) copy-start(f32[1,2,8,128]{3,1,2,0:T(2,128)} %copy-done.32) | copy-start | bytes 24580
  1027.8 25.0 %copy-start.50 = (f32[128]{0:T(128)S(1)}, f32[128]{0:T(128)}, u32[]{:S(2)}) copy-start(f32[128]{0:T(128)} %copy-done.49) | copy-start | bytes 1540
  1027.8 26.7 %copy-start.45 = (f32[2048]{0:T(1024)S(1)}, f32[2048]{0:T(1024)}, u32[]{:S(2)}) copy-start(f32[2048]{0:T(1024)} %get-tuple-element.19) | copy-start | bytes 24580
  1027.8 26.7 %copy-start.59 = (f32[128]{0:T(128)S(1)}, f32[128]{0:T(128)}, u32[]{:S(2)}) copy-start(f32[128]{0:T(128)} %get-tuple-element.13) | copy-start | bytes 1540
  1027.8 26.7 %copy-start.60 = (f32[128]{0:T(128)S(1)}, f32[128]{0:T(128)}, u32[]{:S(2)}) copy-start(f32[128]{0:T(128)} %get-tuple-element.15) | copy-start | bytes 1540
  1027.8 214.8 %copy-start.37 = (f32[1,2,8,128]{3,1,2,0:T(2,128)S(1)}, f32[1,2,8,128]{3,1,2,0:T(2,128)}, u32[]{:S(2)}) copy-start(f32[1,2,8,128]{3,1,2,0:T(2,128)} %copy-done.36) | copy-start | bytes 24580
  1027.8 214.8 %copy-start.56 = (f32[128]{0:T(128)S(1)}, f32[128]{0:T(128)}, u32[]{:S(2)}) copy-start(f32[128]{0:T(128)} %copy-done.55) | copy-start | bytes 1540
  1027.8 214.8 %copy-start.58 = (f32[128]{0:T(128)S(1)}, f32[128]{0:T(128)}, u32[]{:S(2)}) copy-start(f32[128]{0:T(128)} %copy-done.57) | copy-start | bytes 1540
  (43 other events, 132.6 us)
Sparse Core Ops, SparseCore 0:
  15.0 159.9 all-reduce.2
  642.8 184.8 reduce-scatter.7
Sparse Core Ops, SparseCore 1:
  16.9 59.0 all-gather.11
  196.1 46.9 all-gather.15
  269.4 50.3 all-gather.13
  323.3 117.4 all-gather.19
  444.4 112.9 all-gather.17
  833.0 65.5 all-gather.21
  905.4 49.7 reduce-scatter.13
  957.8 57.9 reduce-scatter.11
  1019.2 33.5 reduce-scatter.9
  1055.1 187.4 reduce-scatter.5
  1244.5 32.8 all-gather.25
  1279.4 39.4 all-gather.23
